TPU v7x, 32 devices: a whole 2x2x4 slice. The times are simulated.
32 devices in a mesh: rep: 8 (over z, x), grp: 4 (over y, core).
Axes of the slice: x: 2, y: 2, z: 4, core: 2. Of those that a mesh axis runs over, the one named last changes fastest.
Arguments:
- inputs: bfloat16 [2, 65536, 1152], P(None, ('rep', 'grp')), may hold values from -6 to 6
- out_grads: bfloat16 [2, 65536, 1152], P(None, ('rep', 'grp')), may hold values from -6 to 6
- weights: bfloat16 [2, 1152, 1152], P(None, 'grp'), may hold values from -3 to 3
- biases: bfloat16 [2, 1152], P(None, 'grp'), may hold values from -3 to 3
- errors: float32 [8, 2, 1152, 1152], P('rep', None, 'grp'), may hold values from -6 to 6
- momenta: float32 [2, 1152, 1152], P(None, 'grp'), may hold values from -3 to 3
- bias_momenta: float32 [2, 1152], P(None, 'grp'), may hold values from -3 to 3
- q_start: float32 [2, 1152, 32], replicated, may hold values from -6 to 6
Outputs:
- new_weights: bfloat16 [2, 1152, 1152], replicated
- new_biases: bfloat16 [2, 1152], replicated
- new_errors: float32 [8, 2, 1152, 1152], P('rep', None, 'grp')
- new_momenta: float32 [2, 1152, 1152], P(None, 'grp')
- new_bias_momenta: float32 [2, 1152], P(None, 'grp')
All inputs are finite; a program needn't handle non-finite values.
Results may differ from a plain program's by a relative error of at most 0.0045.
Values may be sent and summed in bfloat16 or wider, within the bound.
A program may use at most 256 MiB of HBM per device.

v0:
```python
import jax
import jax.numpy as jnp
from jax import lax
from jax.sharding import PartitionSpec as P

ROUNDS = 2
NS_STEPS = 5


HIGH = lax.Precision.HIGHEST


def orthonormal(p_sum, gram):
    fro = jnp.sqrt(jnp.sum(gram * gram, axis=(1, 2))) + 1e-06
    scaled = gram / fro[:, None, None]
    eye = jnp.eye(gram.shape[-1], dtype=jnp.float32)
    ymat = scaled
    zmat = jnp.broadcast_to(eye, gram.shape)
    for step in range(NS_STEPS):
        tmat = 1.5 * eye - 0.5 * jnp.einsum("lab,lbc->lac", zmat, ymat, precision=HIGH)
        ymat = jnp.einsum("lab,lbc->lac", ymat, tmat, precision=HIGH)
        zmat = jnp.einsum("lab,lbc->lac", tmat, zmat, precision=HIGH)
    phat = jnp.einsum("lrk,lkj->lrj", p_sum, zmat, precision=HIGH)
    return phat / jnp.sqrt(fro)[:, None, None]


def body(inputs, out_grads, weights, biases, errors, momenta, bias_momenta, q_start):
    layers = inputs.shape[0]
    tok = inputs.shape[1]
    width = inputs.shape[2]
    groups = lax.axis_size("grp")
    reps = lax.axis_size("rep")
    rows = width // groups
    scale = float(tok) ** (-0.5)
    grads = []
    for layer in range(layers):
        x_layer = inputs[layer]
        y_layer = out_grads[layer]

        def term(start, count, x_layer=x_layer, y_layer=y_layer):
            return jnp.einsum("tr,te->re", x_layer, y_layer, preferred_element_type=jnp.float32)

        grads.append(
            lax.psum_scatter(
                term(jnp.int32(0), lax.axis_size("grp") * rows),
                "grp",
                scatter_dimension=0,
                tiled=True,
            )
        )
    merged = jnp.stack(grads) * scale + errors[0]
    col_sums = jnp.sum(out_grads, axis=1, dtype=jnp.float32)
    bias_total = lax.psum(col_sums, ("rep", "grp")) * (scale / reps)
    bias_rows = biases.shape[1]
    bias_grad = lax.dynamic_slice_in_dim(
        bias_total, lax.axis_index("grp") * bias_rows, bias_rows, 1
    )
    qmat = q_start
    phat = None
    for rnd in range(ROUNDS):
        local_p = jnp.einsum("lre,lek->lrk", merged, qmat, precision=HIGH)
        p_sum = lax.psum(local_p, "rep")
        local_gram = jnp.einsum("lrk,lrj->lkj", p_sum, p_sum, precision=HIGH)
        gram = lax.psum(local_gram, "grp")
        phat = orthonormal(p_sum, gram)
        local_q = jnp.einsum("lre,lrk->lek", merged, phat, precision=HIGH)
        qmat = lax.psum(local_q, ("rep", "grp"))
    approx = jnp.einsum("lrk,lek->lre", phat, qmat, precision=HIGH) / reps
    new_errors = (merged - approx)[None]
    new_momenta = 0.9 * momenta + approx
    weight_shard = (weights.astype(jnp.float32) - 0.5 * new_momenta).astype(jnp.bfloat16)
    new_bias_momenta = 0.9 * bias_momenta + bias_grad
    bias_shard = (biases.astype(jnp.float32) - 0.5 * new_bias_momenta).astype(jnp.bfloat16)
    new_weights, new_biases = (
        lax.all_gather(weight_shard, "grp", axis=1, tiled=True),
        lax.all_gather(bias_shard, "grp", axis=1, tiled=True),
    )
    return (new_weights, new_biases, new_errors, new_momenta, new_bias_momenta)


def solution(mesh):
    placed = (
        P(None, ("rep", "grp"), None),
        P(None, ("rep", "grp"), None),
        P(None, "grp", None),
        P(None, "grp"),
        P("rep", None, "grp", None),
        P(None, "grp", None),
        P(None, "grp"),
        P(),
    )
    return jax.shard_map(
        body,
        mesh=mesh,
        in_specs=placed,
        out_specs=(P(), P(), P("rep", None, "grp", None), P(None, "grp", None), P(None, "grp")),
        check_vma=False,
    )
```

profile of v0, /device:TPU:1, one launch (start us, length us, event | category | flops | bytes accessed | tf_op | source)
XLA Modules:
  0.0 638.7 jit_solution(17701296804495009217)
XLA Ops:
  7.2 0.0 reduce-scatter.3.cloned.1.call-start
  7.2 12.5 %fusion.3 = f32[1152,1152]{1,0:T(8,128)} fusion(bf16[2,2048,1152]{2,1,0:T(8,128)(2,1)} %param.9, bf16[2,2048,1152]{2,1,0:T(8,128)(2,1)} %param.8), kind=kOutput, calls=%fused_computation.4 | convolution fusion | flops 5435817984 | bytes 14745600 | tf_op jit(solution)/shard_map/tr,te->re/dot_general | solution.py:41
  19.7 0.0 reduce-scatter.3.cloned.1.call-update
  19.7 0.2 reduce-scatter.5.cloned.1.call-start
  19.9 13.0 %fusion = f32[1152,1152]{1,0:T(8,128)} fusion(bf16[2,2048,1152]{2,1,0:T(8,128)(2,1)} %param.9, bf16[2,2048,1152]{2,1,0:T(8,128)(2,1)} %param.8), kind=kOutput, calls=%fused_computation.1 | convolution fusion | flops 5435817984 | bytes 14745600 | tf_op jit(solution)/shard_map/tr,te->re/dot_general | solution.py:41
  33.0 0.0 all-reduce.5.cloned.1.call-start
  33.0 40.7 %reduce-scatter.3.cloned.1.call-done = f32[288,1152]{1,0:T(8,128)} async-done(((f32[1152,1152]{1,0:T(8,128)}), f32[288,1152]{1,0:T(8,128)}) %reduce-scatter.3.cloned.1.call-update) | async-done | bytes 1327120 | tf_op jit(solution)/shard_map/reduce_scatter | solution.py:44
  73.8 55.2 %reduce-scatter.5.cloned.1.call-done = f32[288,1152]{1,0:T(8,128)} async-done(((f32[1152,1152]{1,0:T(8,128)}), f32[288,1152]{1,0:T(8,128)}) %reduce-scatter.5.cloned.1.call-update) | async-done | bytes 1327120 | tf_op jit(solution)/shard_map/reduce_scatter | solution.py:44
  128.9 2.8 fusion.10
  131.8 3.1 fusion.36
  134.9 0.0 all-reduce.7.cloned.1.call-start
  135.0 67.6 %all-reduce.5.cloned.1.call-done = f32[2,288,32]{1,2,0:T(8,128)} async-done(((f32[2,288,32]{1,2,0:T(8,128)}), f32[2,288,32]{1,2,0:T(8,128)}) %all-reduce.5.cloned.1.call-update) | async-done | bytes 73744 | tf_op jit(solution)/shard_map/psum | solution.py:62
  202.6 1.2 fusion.37
  203.8 12.4 %psum.50 = f32[2,32,32]{2,1,0:T(8,128)S(1)} all-reduce(f32[2,32,32]{2,1,0:T(8,128)S(1)} %fusion.37), channel_id=1, replica_groups=mesh['rep'=8,'grp'=4] {'grp'}, use_global_device_ids=true, to_apply=%region_3.0 | all-reduce | flops 2048 | bytes 16384 | tf_op jit(solution)/shard_map/psum | solution.py:64
  216.2 0.1 multiply_reduce_fusion.1
  216.4 0.2 fusion.20
  216.6 0.2 fusion.29
  216.9 0.2 fusion.24
  217.0 0.2 fusion.19
  217.2 0.2 fusion.39
  217.4 0.2 fusion.38
  217.5 0.2 fusion.18
  217.7 0.2 fusion.41
  217.9 0.2 fusion.40
  218.0 0.2 fusion.17
  218.2 0.2 fusion.43
  218.4 0.2 fusion.42
  218.5 0.2 fusion.16
  218.7 0.2 fusion.44
  219.0 1.1 convolution_divide_fusion.1
  220.1 2.5 fusion.45
  222.6 0.3 all-reduce.9.cloned.1.call-start
  222.9 124.0 %all-reduce.7.cloned.1.call-done = f32[2,1152,32]{1,2,0:T(8,128)} async-done(((f32[2,1152,32]{1,2,0:T(8,128)}), f32[2,1152,32]{1,2,0:T(8,128)}) %all-reduce.7.cloned.1.call-update) | async-done | bytes 294928 | tf_op jit(solution)/shard_map/psum | solution.py:67
  346.8 4.0 fusion.46
  350.9 0.0 all-reduce.11.cloned.1.call-start
  351.0 69.1 %all-reduce.9.cloned.1.call-done = f32[2,288,32]{1,2,0:T(8,128)} async-done(((f32[2,288,32]{1,2,0:T(8,128)}), f32[2,288,32]{1,2,0:T(8,128)}) %all-reduce.9.cloned.1.call-update) | async-done | bytes 73744 | tf_op jit(solution)/shard_map/psum | solution.py:62
  420.1 1.2 fusion.47
  421.3 12.4 %psum.53 = f32[2,32,32]{2,1,0:T(8,128)S(1)} all-reduce(f32[2,32,32]{2,1,0:T(8,128)S(1)} %fusion.47), channel_id=1, replica_groups=mesh['rep'=8,'grp'=4] {'grp'}, use_global_device_ids=true, to_apply=%region_7.0 | all-reduce | flops 2048 | bytes 16384 | tf_op jit(solution)/shard_map/psum | solution.py:64
  433.7 0.1 multiply_reduce_fusion
  433.8 0.2 fusion.15
  434.1 0.2 fusion.30
  434.3 0.2 fusion.21
  434.5 0.2 fusion.14
  434.7 0.2 fusion.49
  434.8 0.2 fusion.48
  435.0 0.2 fusion.13
  435.2 0.2 fusion.51
  435.3 0.2 fusion.50
  435.5 0.2 fusion.12
  435.7 0.2 fusion.53
  435.8 0.2 fusion.52
  436.0 0.2 fusion.11
  436.2 0.2 fusion.54
  436.4 1.1 convolution_divide_fusion
  437.5 2.5 fusion.55
  440.1 0.0 all-gather.3.cloned.1.call-start
  440.1 124.2 %all-reduce.11.cloned.1.call-done = f32[2,1152,32]{1,2,0:T(8,128)} async-done(((f32[2,1152,32]{1,2,0:T(8,128)}), f32[2,1152,32]{1,2,0:T(8,128)}) %all-reduce.11.cloned.1.call-update) | async-done | bytes 294928 | tf_op jit(solution)/shard_map/psum | solution.py:67
  564.3 7.9 %subtract_convert_fusion = (bf16[2,288,1152]{2,1,0:T(8,128)(2,1)}, f32[2,288,1152]{2,1,0:T(8,128)}, f32[1,2,288,1152]{3,2,1,0:T(8,128)}) fusion(bf16[2,288,1152]{2,1,0:T(8,128)(2,1)} %param.10, f32[2,288,1152]{2,1,0:T(8,128)} %param.13, f32[2,288,1152]{2,1,0:T(8,128)S(1)} %fusion.10, f32[2,288,32]{1,2,0:T(8,128)S(1)} %convolution_divide_fusion, ...), kind=kOutput, calls=%fused_computation.15 | convolution fusion | flops 260112384 | bytes 13639680 | tf_op jit(solution)/shard_map/lrk,lek->lre/dot_general | solution.py:68
  572.3 5.0 convert_reduce_fusion
  577.2 41.3 %psum.55 = f32[2,1152]{1,0:T(2,128)S(1)} all-reduce(f32[2,1152]{1,0:T(2,128)S(1)} %convert_reduce_fusion), channel_id=1, replica_groups=mesh['rep'=8,'grp'=4] {'rep','grp'}, use_global_device_ids=true, to_apply=%region_11.0 | all-reduce | flops 2304 | bytes 18432 | tf_op jit(solution)/shard_map/psum | solution.py:53
  618.5 0.7 fusion.32
  619.2 6.7 %all-gather = bf16[4,288,2]{1,2,0:T(2,128)(2,1)S(1)} all-gather(bf16[1,288,2]{1,2,0:T(2,128)(2,1)S(1)} %get-tuple-element.5), channel_id=1, replica_groups=mesh['rep'=8,'grp'=4] {'grp'}, dimensions={0}, use_global_device_ids=true | all-gather | bytes 5760 | tf_op jit(solution)/shard_map/all_gather | solution.py:76
  625.9 0.7 reshape.33
  626.6 5.3 copy.24
  (18 shorter events, 0.2 us)
Async XLA Ops:
  7.2 124.6 %copy-start = (f32[2,1152,32]{1,2,0:T(8,128)S(1)}, f32[2,1152,32]{1,2,0:T(8,128)}, u32[]{:S(2)}) copy-start(f32[2,1152,32]{1,2,0:T(8,128)} %param.15) | copy-start | bytes 884740
  7.2 66.6 %reduce-scatter.3.cloned.1.call-start = ((), (), s32[]{:S(2)}) async-start(), calls=%async_computation.2 | async-start | bytes 6635520 | tf_op jit(solution)/shard_map/reduce_scatter | solution.py:44
  19.7 109.2 %reduce-scatter.5.cloned.1.call-start = ((), (), s32[]{:S(2)}) async-start(), calls=%async_computation.3 | async-start | bytes 6635520 | tf_op jit(solution)/shard_map/reduce_scatter | solution.py:44
  33.0 169.6 %all-reduce.5.cloned.1.call-start = ((), (), s32[]{:S(2)}) async-start(), calls=%async_computation.4 | async-start | bytes 196608 | tf_op jit(solution)/shard_map/psum | solution.py:62
  134.9 211.9 %all-reduce.7.cloned.1.call-start = ((), (), s32[]{:S(2)}) async-start(), calls=%async_computation.5 | async-start | bytes 589824 | tf_op jit(solution)/shard_map/psum | solution.py:67
  222.6 197.5 %all-reduce.9.cloned.1.call-start = ((), (), s32[]{:S(2)}) async-start(), calls=%async_computation.6 | async-start | bytes 196608 | tf_op jit(solution)/shard_map/psum | solution.py:62
  350.9 213.4 %all-reduce.11.cloned.1.call-start = ((), (), s32[]{:S(2)}) async-start(), calls=%async_computation.7 | async-start | bytes 589824 | tf_op jit(solution)/shard_map/psum | solution.py:67
  440.1 186.6 %all-gather.3.cloned.1.call-start = ((), (), s32[]{:S(2)}) async-start(), calls=%async_computation.8 | async-start | bytes 6635520 | tf_op jit(solution)/shard_map/all_gather | solution.py:75
  572.2 46.3 %copy-start.1 = (f32[2,288]{1,0:T(2,128)S(1)}, f32[2,288]{1,0:T(2,128)}, u32[]{:S(2)}) copy-start(f32[2,288]{1,0:T(2,128)} %param.14) | copy-start | bytes 6916
  572.2 46.3 %copy-start.2 = (bf16[2,288]{1,0:T(2,128)(2,1)S(1)}, bf16[2,288]{1,0:T(2,128)(2,1)}, u32[]{:S(2)}) copy-start(bf16[2,288]{1,0:T(2,128)(2,1)} %param.11) | copy-start | bytes 3460
Sparse Core Ops, SparseCore 0:
  19.8 53.8 reduce-scatter.2
  77.1 51.8 reduce-scatter.4
  135.0 67.5 all-reduce.4
  222.7 124.0 all-reduce.6
  351.0 69.0 all-reduce.8
  440.2 124.0 all-reduce.10
  572.4 43.4 all-gather.2
where the time goes:
time: 639 us
  waiting for transfers between devices  481 us (75%)
  blocking collectives  72.9 us (11%)
  matrix products  55.1 us (9%)
  between operations  14.5 us (2%)
  other arithmetic  8.73 us (1%)
    psum x2, waiting for transfers between devices, body(): qmat = lax.psum(local_q, ('rep', 'grp'))  248 us
    psum x2, waiting for transfers between devices, body(): p_sum = lax.psum(local_p, 'rep')  137 us
    reduce_scatter x2, waiting for transfers between devices, body(): lax.psum_scatter(term(jnp.int32(0), lax.axis_size('grp') * rows), 'grp',...  95.9 us
    psum x1, blocking collectives, body(): bias_total = lax.psum(col_sums, ('rep', 'grp')) * (scale / reps)  41.3 us
    dot_general x2, matrix products, term(): jnp.einsum('tr,te->re', x_layer, y_layer, preferred_element_type=jnp.floa...  25.5 us
    psum x2, blocking collectives, body(): gram = lax.psum(local_gram, 'grp')  24.9 us
  transfers between devices with their start and end apart: 7, of which 6 were waited for; matrix products, arithmetic and copies ran while one was open for 3% of the time, Pallas kernels for 0%

commit v1 on v0

v1 whole, which is shorter than its diff:
```python
import functools

import jax
import jax.numpy as jnp
from jax import lax
from jax.experimental import pallas as pl
from jax.experimental.pallas import tpu as pltpu
from jax.sharding import PartitionSpec as P

ROUNDS = 2
NS_STEPS = 5
HIGH = lax.Precision.HIGHEST
F32 = jnp.float32
BF16 = jnp.bfloat16
NN = (((1,), (0,)), ((), ()))
NT = (((1,), (1,)), ((), ()))
TN = (((0,), (0,)), ((), ()))


def dot(a, b, dims, precision=None):
    return lax.dot_general(a, b, dims, precision=precision, preferred_element_type=F32)


def split(a):
    hi = a.astype(BF16)
    return hi, (a - hi.astype(F32)).astype(BF16)


def step_kernel(sizes, x_hbm, y_hbm, errors, weights, momenta, q0, bias_in,
                merged, phat_out, q_out, w_out, bias_out, small_out,
                xbuf, ybuf, gfull, gsend, grecv, ysend, yrecv, mhi, mlo, wown,
                psend, prs, pfull, tsend, trs, tmid, trr, tag, brep, bgrp, bsmall,
                load_sem, s_core, r_core, s_y, r_y, s_wc, r_wc, s_rep, r_rep, s_grp, r_grp):
    L, G, R, rank, width, tok, chunk = sizes
    rows = width // G
    K = L * rank
    Y = G // 2
    pp = psend.shape[2]
    pr = tsend.shape[3]
    scale = float(tok) ** (-0.5)
    me_r = lax.axis_index("rep")
    me_g = lax.axis_index("grp")
    core = lax.rem(me_g, 2)
    yy = lax.div(me_g, 2)
    mate = me_g + 1 - 2 * core

    loads = []
    for l in range(L):
        for which, (src, dst) in enumerate(((x_hbm, xbuf), (y_hbm, ybuf))):
            loads.append(pltpu.make_async_copy(src.at[l], dst.at[l], load_sem.at[2 * l + which]))
            loads[-1].start()

    barrier = pltpu.get_barrier_semaphore()
    for d in range(1, R):
        pl.semaphore_signal(barrier, inc=1, device_id={"rep": lax.rem(me_r + d, R)},
                            device_id_type=pl.DeviceIdType.MESH)
    for d in range(1, G):
        pl.semaphore_signal(barrier, inc=1, device_id={"grp": lax.rem(me_g + d, G)},
                            device_id_type=pl.DeviceIdType.MESH)
    pl.semaphore_wait(barrier, R + G - 2)

    def remote(src, dst, send, recv, axis, peer):
        copy = pltpu.make_async_remote_copy(
            src_ref=src, dst_ref=dst, send_sem=send, recv_sem=recv,
            device_id={axis: peer}, device_id_type=pl.DeviceIdType.MESH)
        copy.start()
        return copy

    def over_rep(phase, src, dst):
        return [remote(src(lax.rem(me_r + d, R)), dst, s_rep.at[phase, d - 1], r_rep.at[phase, d - 1],
                       "rep", lax.rem(me_r + d, R)) for d in range(1, R)]

    def over_grp(phase, src, dst):
        return [remote(src(lax.rem(me_g + d, G)), dst, s_grp.at[phase, d - 1], r_grp.at[phase, d - 1],
                       "grp", lax.rem(me_g + d, G)) for d in range(1, G)]

    def wait(copies):
        for copy in copies:
            copy.wait_recv()
        for copy in copies:
            copy.wait_send()

    def row_ds(g):
        return pl.ds(pl.multiple_of(g * rows, 16), rows)

    bsmall[me_g] = bias_in[...]
    small_copies = over_grp(0, lambda g: bsmall.at[me_g], bsmall.at[me_g])

    def grads(l):
        loads[2 * l].wait()
        loads[2 * l + 1].wait()

        def one(j, carry):
            at = pl.ds(pl.multiple_of(j * chunk, 128), chunk)
            gfull[l, at, :] = dot(xbuf[l, :, at], ybuf[l], TN)
            return carry

        lax.fori_loop(0, width // chunk, one, 0)
        for y in range(Y):
            gsend[l, y] = gfull[l, row_ds(2 * y + 1 - core), :].astype(BF16)
        return remote(gsend.at[l], grecv.at[l], s_core.at[l], r_core.at[l], "grp", mate)

    def to_y(l, core_copy):
        core_copy.wait_recv()
        copies = []
        for d in range(1, Y):
            y = lax.rem(yy + d, Y)
            ysend[l, d - 1] = (gfull[l, row_ds(2 * y + core), :] + grecv[l, y].astype(F32)).astype(BF16)
            copies.append(remote(ysend.at[l, d - 1], yrecv.at[l, d - 1], s_y.at[l, d - 1],
                                 r_y.at[l, d - 1], "grp", 2 * y + core))
        return copies

    core_copies, y_copies = [], []
    for l in range(L):
        core_copies.append(grads(l))
        if l > 0:
            y_copies.append(to_y(l - 1, core_copies[l - 1]))
    for l in range(L):
        total = dot(jnp.ones((8, tok), BF16), ybuf[l], NN)
        brep[me_r, pl.ds(l, 1), :] = total[:1]
    bias_copies = over_rep(0, lambda r: brep.at[me_r], brep.at[me_r])
    y_copies.append(to_y(L - 1, core_copies[L - 1]))
    for l in range(L):
        wown[l] = (weights[l].astype(F32) - 0.45 * momenta[l]).astype(BF16)
    wait(bias_copies)
    bgrp[me_g] = jnp.sum(brep[...], axis=0)
    bias_copies = over_grp(1, lambda g: bgrp.at[me_g], bgrp.at[me_g])
    local_w = pltpu.make_async_copy(wown, w_out.at[me_g], load_sem.at[2 * L])
    local_w.start()
    for l in range(L):
        for copy in y_copies[l]:
            copy.wait_recv()
        total = gfull[l, row_ds(me_g), :] + grecv[l, yy].astype(F32)
        for d in range(1, Y):
            total = total + yrecv[l, d - 1].astype(F32)
        m = total * scale + errors[l]
        merged[l] = m
        hi, lo = split(m)
        mhi[l] = hi
        mlo[l] = lo
    w_copies = [remote(wown, w_out.at[me_g], s_wc.at[d - 1], r_wc.at[d - 1], "grp",
                       lax.rem(me_g + d, G)) for d in range(1, G)]

    def apply(a, l, dims):
        hi, lo = split(a)
        both = dot(jnp.concatenate([hi, lo], axis=0), mhi[l], dims)
        return both[:rank] + both[rank:] + dot(hi, mlo[l], dims)

    row = lax.broadcasted_iota(jnp.int32, (K, K), 0)
    col = lax.broadcasted_iota(jnp.int32, (K, K), 1)
    same = (lax.div(row, rank) == lax.div(col, rank)).astype(F32)
    eye = (row == col).astype(F32)
    layer_of = lax.div(lax.broadcasted_iota(jnp.int32, (K, 1), 0), rank)

    q = [q0[l] for l in range(L)]
    for rnd in range(ROUNDS):
        p = jnp.concatenate([apply(q[l], l, NT) for l in range(L)], axis=0)
        for r in range(R):
            if r * pp < K:
                psend[rnd, r] = p[r * pp:(r + 1) * pp]
        prs[rnd, me_r] = psend[rnd, me_r]
        wait(over_rep(1 + 4 * rnd, lambda r: psend.at[rnd, r], prs.at[rnd, me_r]))
        pfull[rnd, me_g, me_r] = jnp.sum(prs[rnd], axis=0)
        wait(over_rep(2 + 4 * rnd, lambda r: pfull.at[rnd, me_g, me_r], pfull.at[rnd, me_g, me_r]))
        p_copies = over_grp(2 + 3 * rnd, lambda g: pfull.at[rnd, me_g], pfull.at[rnd, me_g])

        def whole_p(g):
            return jnp.concatenate([pfull[rnd, g, r] for r in range(R)], axis=0)[:K]

        p = whole_p(me_g)
        t = jnp.concatenate([apply(p[l * rank:(l + 1) * rank], l, NN) for l in range(L)], axis=0)
        for i in range(G * R):
            if i * pr < K:
                tsend[rnd, i // R, i % R] = t[i * pr:(i + 1) * pr]
        trs[rnd, me_g] = tsend[rnd, me_g]
        copies = over_grp(3 + 3 * rnd, lambda g: tsend.at[rnd, g], trs.at[rnd, me_g])

        wait(p_copies)
        gram = jnp.zeros((K, K), F32)
        for g in range(G):
            pg = whole_p(g)
            gram = gram + dot(pg, pg, NT, HIGH)
        gram = gram * same
        squares = jnp.sum(gram * gram, axis=1, keepdims=True)
        fro = jnp.zeros((K, 1), F32)
        for l in range(L):
            mine = layer_of == l
            one = jnp.sum(jnp.where(mine, squares, 0.0), axis=0, keepdims=True)
            fro = jnp.where(mine, jnp.sqrt(one) + 1e-06, fro)
        ymat, zmat = gram / fro, eye

        def newton(ymat, zmat, count):
            for _ in range(count):
                tmat = 1.5 * eye - 0.5 * dot(zmat, ymat, NN, HIGH)
                ymat = dot(ymat, tmat, NN, HIGH)
                zmat = dot(tmat, zmat, NN, HIGH)
            return ymat, zmat

        ymat, zmat = newton(ymat, zmat, 1)
        wait(copies)
        tmid[rnd] = jnp.sum(trs[rnd], axis=0)
        trr[rnd, me_r] = tmid[rnd, me_r]
        copies = over_rep(3 + 4 * rnd, lambda r: tmid.at[rnd, r], trr.at[rnd, me_r])
        ymat, zmat = newton(ymat, zmat, 2)
        wait(copies)
        tag[rnd, me_g, me_r] = jnp.sum(trr[rnd], axis=0)
        copies = over_rep(4 + 4 * rnd, lambda r: tag.at[rnd, me_g, me_r], tag.at[rnd, me_g, me_r])
        ymat, zmat = newton(ymat, zmat, NS_STEPS - 3)
        wait(copies)
        wait(over_grp(4 + 3 * rnd, lambda g: tag.at[rnd, me_g], tag.at[rnd, me_g]))
        t = jnp.concatenate([tag[rnd, i // R, i % R] for i in range(G * R)], axis=0)[:K]
        inv = 1.0 / jnp.sqrt(fro)
        qall = dot(zmat, t, TN, HIGH) * inv
        q = [qall[l * rank:(l + 1) * rank] for l in range(L)]
        if rnd == ROUNDS - 1:
            q_out[...] = qall
            for g in range(G):
                phat_out[g] = dot(zmat, whole_p(g), TN, HIGH) * inv

    wait(bias_copies)
    wait(small_copies)
    bias_out[...] = jnp.sum(bgrp[...], axis=0)
    small_out[...] = bsmall[...]
    for l in range(L):
        core_copies[l].wait_send()
        for copy in y_copies[l]:
            copy.wait_send()
    local_w.wait()
    wait(w_copies)


def factors(ph, q):
    ph_hi, ph_lo = split(ph)
    q_hi, q_lo = split(q)
    return dot(jnp.concatenate([ph_hi, ph_hi, ph_lo], axis=0),
               jnp.concatenate([q_hi, q_lo, q_hi], axis=0), TN)


def weights_kernel(reps, ph, q, w, out):
    approx = factors(ph[0, 0], q[0]) / reps
    out[0] = (w[0, 0].astype(F32) - 0.5 * approx).astype(BF16)


def state_kernel(reps, ph, q, merged, momenta, errors_out, momenta_out):
    approx = factors(ph[0], q[0]) / reps
    errors_out[0] = merged[0] - approx
    momenta_out[0] = 0.9 * momenta[0] + approx


def body(inputs, out_grads, weights, biases, errors, momenta, bias_momenta, q_start):
    L, tok, width = inputs.shape
    G = lax.axis_size("grp")
    R = lax.axis_size("rep")
    rows = width // G
    rank = q_start.shape[2]
    K = L * rank
    Y = G // 2
    scale = float(tok) ** (-0.5)
    pp = -(-K // R)
    pr = -(-K // (G * R))
    chunk = 384 if width % 384 == 0 else 128
    bias_in = jnp.concatenate([bias_momenta, biases.astype(F32)], axis=0)
    vm = pl.BlockSpec(memory_space=pltpu.VMEM)
    hbm = pl.BlockSpec(memory_space=pl.ANY)
    dma = pltpu.SemaphoreType.DMA
    n_rep, n_grp = 1 + 4 * ROUNDS, 2 + 3 * ROUNDS
    merged, phat, q, w_all, bias_sum, small = pl.pallas_call(
        functools.partial(step_kernel, (L, G, R, rank, width, tok, chunk)),
        out_shape=(
            jax.ShapeDtypeStruct((L, rows, width), F32),
            jax.ShapeDtypeStruct((G, K, rows), F32),
            jax.ShapeDtypeStruct((K, width), F32),
            jax.ShapeDtypeStruct((G, L, rows, width), BF16),
            jax.ShapeDtypeStruct((L, width), F32),
            jax.ShapeDtypeStruct((G, 2 * L, rows), F32),
        ),
        in_specs=[hbm, hbm, vm, vm, vm, vm, vm],
        out_specs=(vm, vm, vm, hbm, vm, vm),
        scratch_shapes=[
            pltpu.VMEM((L, tok, width), BF16),
            pltpu.VMEM((L, tok, width), BF16),
            pltpu.VMEM((L, width, width), F32),
            pltpu.VMEM((L, Y, rows, width), BF16),
            pltpu.VMEM((L, Y, rows, width), BF16),
            pltpu.VMEM((L, Y - 1, rows, width), BF16),
            pltpu.VMEM((L, Y - 1, rows, width), BF16),
            pltpu.VMEM((L, rows, width), BF16),
            pltpu.VMEM((L, rows, width), BF16),
            pltpu.VMEM((L, rows, width), BF16),
            pltpu.VMEM((ROUNDS, R, pp, rows), F32),
            pltpu.VMEM((ROUNDS, R, pp, rows), F32),
            pltpu.VMEM((ROUNDS, G, R, pp, rows), F32),
            pltpu.VMEM((ROUNDS, G, R, pr, width), F32),
            pltpu.VMEM((ROUNDS, G, R, pr, width), F32),
            pltpu.VMEM((ROUNDS, R, pr, width), F32),
            pltpu.VMEM((ROUNDS, R, pr, width), F32),
            pltpu.VMEM((ROUNDS, G, R, pr, width), F32),
            pltpu.VMEM((R, L, width), F32),
            pltpu.VMEM((G, L, width), F32),
            pltpu.VMEM((G, 2 * L, rows), F32),
            dma((2 * L + 1,)),
            dma((L,)), dma((L,)),
            dma((L, Y - 1)), dma((L, Y - 1)),
            dma((G - 1,)), dma((G - 1,)),
            dma((n_rep, R - 1)), dma((n_rep, R - 1)),
            dma((n_grp, G - 1)), dma((n_grp, G - 1)),
        ],
        compiler_params=pltpu.CompilerParams(
            collective_id=0, has_side_effects=True, vmem_limit_bytes=62 * 2**20),
        cost_estimate=pl.CostEstimate(
            flops=2 * L * tok * width * width, bytes_accessed=4 * L * tok * width, transcendentals=0),
    )(inputs, out_grads, errors[0], weights, momenta, jnp.swapaxes(q_start, 1, 2), bias_in)

    new_weights = pl.pallas_call(
        functools.partial(weights_kernel, R),
        out_shape=jax.ShapeDtypeStruct((L, width, width), BF16),
        grid=(L, G),
        in_specs=[
            pl.BlockSpec((1, 1, rank, rows), lambda l, g: (g, l, 0, 0)),
            pl.BlockSpec((1, rank, width), lambda l, g: (l, 0, 0)),
            pl.BlockSpec((1, 1, rows, width), lambda l, g: (g, l, 0, 0)),
        ],
        out_specs=pl.BlockSpec((1, rows, width), lambda l, g: (l, g, 0)),
        compiler_params=pltpu.CompilerParams(vmem_limit_bytes=32 * 2**20),
    )(phat.reshape(G, L, rank, rows), q.reshape(L, rank, width), w_all)

    own = lax.dynamic_index_in_dim(phat, lax.axis_index("grp"), 0, keepdims=False)
    block = pl.BlockSpec((1, rows, width), lambda l: (l, 0, 0))
    new_errors, new_momenta = pl.pallas_call(
        functools.partial(state_kernel, R),
        out_shape=(jax.ShapeDtypeStruct((L, rows, width), F32),) * 2,
        grid=(L,),
        in_specs=[
            pl.BlockSpec((1, rank, rows), lambda l: (l, 0, 0)),
            pl.BlockSpec((1, rank, width), lambda l: (l, 0, 0)),
            block, block,
        ],
        out_specs=(block, block),
        compiler_params=pltpu.CompilerParams(vmem_limit_bytes=32 * 2**20),
    )(own.reshape(L, rank, rows), q.reshape(L, rank, width), merged, momenta)

    bias_grad = bias_sum * (scale / R)
    full = jnp.swapaxes(small, 0, 1).reshape(2 * L, width)
    bias_m = 0.9 * full[:L] + bias_grad
    new_biases = (full[L:] - 0.5 * bias_m).astype(BF16)
    new_bias_momenta = lax.dynamic_slice_in_dim(bias_m, lax.axis_index("grp") * rows, rows, 1)
    return (new_weights, new_biases, new_errors[None], new_momenta, new_bias_momenta)


def solution(mesh):
    placed = (
        P(None, ("rep", "grp"), None),
        P(None, ("rep", "grp"), None),
        P(None, "grp", None),
        P(None, "grp"),
        P("rep", None, "grp", None),
        P(None, "grp", None),
        P(None, "grp"),
        P(),
    )
    return jax.shard_map(
        body,
        mesh=mesh,
        in_specs=placed,
        out_specs=(P(), P(), P("rep", None, "grp", None), P(None, "grp", None), P(None, "grp")),
        check_vma=False,
    )
```

time: 639 us -> 190 us (0.30)
  waiting for transfers between devices: 481 us -> 0 us
  Pallas kernels: 0 us -> 178 us
  blocking collectives: 72.9 us -> 0 us
  matrix products: 55.1 us -> 0 us
  between operations: 14.5 us -> 0.71 us
    psum x4 -> x0, waiting for transfers between devices: 385 us -> none  [the longest x2 248 us: body(): qmat = lax.psum(local_q, ('rep', 'grp'))]
    pallas_call x0 -> x3, Pallas kernels: none -> 178 us  [the longest x1 170 us: body(): pl.pallas_call(functools.partial(step_kernel, (L, G, R, rank, width, tok,...]
    reduce_scatter x2 -> x0, waiting for transfers between devices: 95.9 us -> none  [body(): lax.psum_scatter(term(jnp.int32(0), lax.axis_size('grp') * rows), 'grp',...]
    psum x3 -> x0, blocking collectives: 66.2 us -> none  [the longest x1 41.3 us: body(): bias_total = lax.psum(col_sums, ('rep', 'grp')) * (scale / reps)]
    dot_general x39 -> x0, matrix products: 55.1 us -> none  [the longest x2 25.5 us: term(): jnp.einsum('tr,te->re', x_layer, y_layer, preferred_element_type=jnp.floa...]
    all_gather x1 -> x0, blocking collectives: 6.71 us -> none  [body(): lax.all_gather(bias_shard, 'grp', axis=1, tiled=True)]
  transfers between devices with their start and end apart: 7 -> 0, of which waited for: 6 -> 0; matrix products, arithmetic and copies ran while one was open for 3% -> 0% of each run, Pallas kernels for 0% -> 0%
where the time goes in v1:
time: 190 us; the launch traced here: 189 us
  Pallas kernels  178 us (94%)
  local copies, waits for them, and re-layouts  7.95 us (4%)
  other arithmetic  2.59 us (1%)
    pallas_call x1, Pallas kernels, body(): pl.pallas_call(functools.partial(step_kernel, (L, G, R, rank, width, tok,...  170 us
    unnamed x16, local copies, waits for them, and re-layouts  6.21 us
    pallas_call x1, Pallas kernels, body(): pl.pallas_call(functools.partial(weights_kernel, R), out_shape=jax.ShapeD...  5.36 us

profile of v1, /device:TPU:1, one launch (start us, length us, event | category | flops | bytes accessed | tf_op | source)
XLA Modules:
  0.0 189.2 jit_solution(13008584175506808605)
XLA Ops:
  0.6 0.7 convert_element_type.6
  1.3 1.3 pad_maximum_fusion.bias_in
  2.6 169.8 %shard_map.119 = (f32[2,288,1152]{2,1,0:T(8,128)}, f32[4,64,288]{2,1,0:T(8,128)}, f32[64,1152]{1,0:T(8,128)}, bf16[4,2,288,1152]{3,2,1,0:T(8,128)(2,1)}, f32[2,1152]{1,0:T(2,128)}, /*index=5*/f32[4,4,288]{2,1,0:T(4,128)}) custom-call(bf16[2,2048,1152]{2,1,0:T(8,128)(2,1)} %x_hbm.1, bf16[2,2048,1152]{2,1,0:T(8,128)(2,1)} %y_hbm.1, f32[2,288,1152]{2,1,0:T(8,128)} %bitcast.12, ...), custom_call_target="tpu_custom_call" | custom-call | flops 10871635968 | bytes 18874368 | tf_op jit(solution)/shard_map/pallas_call | solution.py:267
  172.4 0.0 copy-start
  172.4 2.5 %copy-done = bf16[4,2,288,1152]{3,2,1,0:T(8,128)(2,1)S(1)} copy-done((bf16[4,2,288,1152]{3,2,1,0:T(8,128)(2,1)S(1)}, bf16[4,2,288,1152]{3,2,1,0:T(8,128)(2,1)}, u32[]{:S(2)}) %copy-start) | copy-done | bytes 5308440
  174.9 0.0 copy-start.3
  174.9 1.0 copy-done.3
  175.9 0.0 copy-start.5
  175.9 1.0 copy-done.5
  176.9 0.0 copy-start.6
  176.9 0.0 copy-start.7
  176.9 0.0 copy-start.1
  176.9 0.0 copy-start.4
  176.9 5.4 %shard_map.120 = bf16[2,1152,1152]{2,1,0:T(8,128)(2,1)} custom-call(f32[4,2,32,288]{3,2,1,0:T(8,128)S(1)} %bitcast.9, f32[2,32,1152]{2,1,0:T(8,128)S(1)} %bitcast.7, bf16[4,2,288,1152]{3,2,1,0:T(8,128)(2,1)S(1)} %copy-done), custom_call_target="tpu_custom_call" | custom-call | tf_op jit(solution)/shard_map/pallas_call | solution.py:314
  182.3 0.0 copy-done.6
  182.3 0.1 slice.11
  182.4 0.1 mul.26
  182.5 0.0 copy-done.7
  182.5 0.6 subtract_convert_fusion
  183.1 0.9 constant_dynamic-slice_fusion.1
  184.0 0.0 copy-done.1
  184.0 0.0 copy-done.4
  184.0 0.0 copy-start.2
  184.0 1.7 copy-done.2
  185.8 2.8 %shard_map.121 = (f32[2,288,1152]{2,1,0:T(8,128)}, f32[2,288,1152]{2,1,0:T(8,128)}) custom-call(f32[2,32,288]{2,1,0:T(8,128)S(1)} %bitcast.10, f32[2,32,1152]{2,1,0:T(8,128)S(1)} %bitcast.8, f32[2,288,1152]{2,1,0:T(8,128)S(1)} %copy-done.2, f32[2,288,1152]{2,1,0:T(8,128)S(1)} %copy-done.1), custom_call_target="tpu_custom_call" | custom-call | tf_op jit(solution)/shard_map/pallas_call | solution.py:329
  188.6 0.7 constant_dynamic-slice_fusion
  (3 shorter events, 0.0 us)
Async XLA Ops:
  172.4 2.5 %copy-start = (bf16[4,2,288,1152]{3,2,1,0:T(8,128)(2,1)S(1)}, bf16[4,2,288,1152]{3,2,1,0:T(8,128)(2,1)}, u32[]{:S(2)}) copy-start(bf16[4,2,288,1152]{3,2,1,0:T(8,128)(2,1)} %get-tuple-element.15.w) | copy-start | bytes 15925252
  174.9 1.0 copy-start.3
  175.9 1.0 copy-start.5
  176.9 5.4 %copy-start.6 = (f32[4,4,288]{2,1,0:T(4,128)S(1)}, f32[4,4,288]{2,1,0:T(4,128)}, u32[]{:S(2)}) copy-start(f32[4,4,288]{2,1,0:T(4,128)} %get-tuple-element.16) | copy-start | bytes 55300
  176.9 5.6 %copy-start.7 = (f32[2,1152]{1,0:T(2,128)S(1)}, f32[2,1152]{1,0:T(2,128)}, u32[]{:S(2)}) copy-start(f32[2,1152]{1,0:T(2,128)} %get-tuple-element.17) | copy-start | bytes 27652
  176.9 7.1 %copy-start.1 = (f32[2,288,1152]{2,1,0:T(8,128)S(1)}, f32[2,288,1152]{2,1,0:T(8,128)}, u32[]{:S(2)}) copy-start(f32[2,288,1152]{2,1,0:T(8,128)} %momenta.3) | copy-start | bytes 7962628
  176.9 7.1 %copy-start.4 = (f32[64,1152]{1,0:T(8,128)S(1)}, f32[64,1152]{1,0:T(8,128)}, u32[]{:S(2)}) copy-start(f32[64,1152]{1,0:T(8,128)} %get-tuple-element.14) | copy-start | bytes 884740
  184.0 1.8 copy-start.2

commit v2 on v1

--- a/solution.py
+++ b/solution.py
@@ -9,7 +9,6 @@
 
 ROUNDS = 2
 NS_STEPS = 5
-HIGH = lax.Precision.HIGHEST
 F32 = jnp.float32
 BF16 = jnp.bfloat16
 NN = (((1,), (0,)), ((), ()))
@@ -26,12 +25,26 @@
     return hi, (a - hi.astype(F32)).astype(BF16)
 
 
+def dot3(a, b):
+    a_hi, a_lo = split(a)
+    b_hi, b_lo = split(b)
+    return dot(jnp.concatenate([a_hi, a_hi, a_lo], axis=1),
+               jnp.concatenate([b_hi, b_lo, b_hi], axis=0), NN)
+
+
+def factors(ph, q):
+    ph_hi, ph_lo = split(ph)
+    q_hi, q_lo = split(q)
+    return dot(jnp.concatenate([ph_hi, ph_hi, ph_lo], axis=0),
+               jnp.concatenate([q_hi, q_lo, q_hi], axis=0), TN)
+
+
 def step_kernel(sizes, x_hbm, y_hbm, errors, weights, momenta, q0, bias_in,
                 merged, phat_out, q_out, w_out, bias_out, small_out,
                 xbuf, ybuf, gfull, gsend, grecv, ysend, yrecv, mhi, mlo, wown,
                 psend, prs, pfull, tsend, trs, tmid, trr, tag, brep, bgrp, bsmall,
                 load_sem, s_core, r_core, s_y, r_y, s_wc, r_wc, s_rep, r_rep, s_grp, r_grp):
-    L, G, R, rank, width, tok, chunk = sizes
+    L, G, R, rank, width, tok, chunk, pieces = sizes
     rows = width // G
     K = L * rank
     Y = G // 2
@@ -83,63 +96,93 @@
     def row_ds(g):
         return pl.ds(pl.multiple_of(g * rows, 16), rows)
 
+    half = lax.rem(me_r, 2)
+    pair = me_r + 1 - 2 * half
+    hl = L // 2
+    first = pl.ds(half * hl, hl)
+    second = pl.ds((1 - half) * hl, hl)
+    for l in range(L):
+        wown[l] = (weights[l].astype(F32) - 0.45 * momenta[l]).astype(BF16)
+    w_y = [remote(wown.at[first], w_out.at[me_g, first], s_wc.at[0, d], r_wc.at[0, d], "grp",
+                  2 * lax.rem(yy + d, Y) + core) for d in range(1, Y)]
+    w_rest = [remote(wown, w_out.at[me_g], s_wc.at[0, 0], r_wc.at[0, 0], "grp", mate)]
+    local_w = pltpu.make_async_copy(wown, w_out.at[me_g], load_sem.at[2 * L])
+    local_w.start()
+
+    def w_forward():
+        copies = []
+        for d in range(1, Y):
+            w_y[d - 1].wait_recv()
+            got = w_out.at[2 * lax.rem(yy + Y - d, Y) + core, first]
+            copies.append(remote(got, got, s_wc.at[1, d], r_wc.at[1, d], "rep", pair))
+            w_rest.append(remote(got, got, s_wc.at[2, d], r_wc.at[2, d], "grp", mate))
+        return copies
+
+    def w_last(copies):
+        for d in range(1, Y):
+            copies[d - 1].wait_recv()
+            got = w_out.at[2 * lax.rem(yy + Y - d, Y) + core, second]
+            w_rest.append(remote(got, got, s_wc.at[3, d], r_wc.at[3, d], "grp", mate))
+
     bsmall[me_g] = bias_in[...]
     small_copies = over_grp(0, lambda g: bsmall.at[me_g], bsmall.at[me_g])
 
-    def grads(l):
-        loads[2 * l].wait()
-        loads[2 * l + 1].wait()
+    def grads(u):
+        l, at = units[u]
+        w = at.size
+        if at.start == 0:
+            loads[2 * l].wait()
+            loads[2 * l + 1].wait()
 
         def one(j, carry):
-            at = pl.ds(pl.multiple_of(j * chunk, 128), chunk)
-            gfull[l, at, :] = dot(xbuf[l, :, at], ybuf[l], TN)
+            lines = pl.ds(pl.multiple_of(j * chunk, 128), chunk)
+            gfull[l, lines, at] = dot(xbuf[l, :, lines], ybuf[l, :, at], TN)
             return carry
 
         lax.fori_loop(0, width // chunk, one, 0)
         for y in range(Y):
-            gsend[l, y] = gfull[l, row_ds(2 * y + 1 - core), :].astype(BF16)
-        return remote(gsend.at[l], grecv.at[l], s_core.at[l], r_core.at[l], "grp", mate)
-
-    def to_y(l, core_copy):
-        core_copy.wait_recv()
+            gsend[l, y, :, at] = gfull[l, row_ds(2 * y + 1 - core), at].astype(BF16)
+        return remote(gsend.at[l, :, :, at], grecv.at[l, :, :, at], s_core.at[u], r_core.at[u],
+                      "grp", mate)
+
+    def to_y(u):
+        l, at = units[u]
+        core_copies[u].wait_recv()
         copies = []
         for d in range(1, Y):
             y = lax.rem(yy + d, Y)
-            ysend[l, d - 1] = (gfull[l, row_ds(2 * y + core), :] + grecv[l, y].astype(F32)).astype(BF16)
-            copies.append(remote(ysend.at[l, d - 1], yrecv.at[l, d - 1], s_y.at[l, d - 1],
-                                 r_y.at[l, d - 1], "grp", 2 * y + core))
+            ysend[l, d - 1, :, at] = (gfull[l, row_ds(2 * y + core), at]
+                                      + grecv[l, y, :, at].astype(F32)).astype(BF16)
+            copies.append(remote(ysend.at[l, d - 1, :, at], yrecv.at[l, d - 1, :, at],
+                                 s_y.at[u, d - 1], r_y.at[u, d - 1], "grp", 2 * y + core))
         return copies
 
+    units = [(l, pl.ds(start, size)) for l in range(L) for start, size in pieces]
     core_copies, y_copies = [], []
-    for l in range(L):
-        core_copies.append(grads(l))
-        if l > 0:
-            y_copies.append(to_y(l - 1, core_copies[l - 1]))
+    for u in range(len(units)):
+        core_copies.append(grads(u))
+        if u > 0:
+            y_copies.append(to_y(u - 1))
+    y_copies.append(to_y(len(units) - 1))
     for l in range(L):
         total = dot(jnp.ones((8, tok), BF16), ybuf[l], NN)
         brep[me_r, pl.ds(l, 1), :] = total[:1]
     bias_copies = over_rep(0, lambda r: brep.at[me_r], brep.at[me_r])
-    y_copies.append(to_y(L - 1, core_copies[L - 1]))
-    for l in range(L):
-        wown[l] = (weights[l].astype(F32) - 0.45 * momenta[l]).astype(BF16)
+    w_x = w_forward()
     wait(bias_copies)
     bgrp[me_g] = jnp.sum(brep[...], axis=0)
     bias_copies = over_grp(1, lambda g: bgrp.at[me_g], bgrp.at[me_g])
-    local_w = pltpu.make_async_copy(wown, w_out.at[me_g], load_sem.at[2 * L])
-    local_w.start()
-    for l in range(L):
-        for copy in y_copies[l]:
+    for u, (l, at) in enumerate(units):
+        for copy in y_copies[u]:
             copy.wait_recv()
-        total = gfull[l, row_ds(me_g), :] + grecv[l, yy].astype(F32)
+        total = gfull[l, row_ds(me_g), at] + grecv[l, yy, :, at].astype(F32)
         for d in range(1, Y):
-            total = total + yrecv[l, d - 1].astype(F32)
-        m = total * scale + errors[l]
-        merged[l] = m
+            total = total + yrecv[l, d - 1, :, at].astype(F32)
+        m = total * scale + errors[l, :, at]
+        merged[l, :, at] = m
         hi, lo = split(m)
-        mhi[l] = hi
-        mlo[l] = lo
-    w_copies = [remote(wown, w_out.at[me_g], s_wc.at[d - 1], r_wc.at[d - 1], "grp",
-                       lax.rem(me_g + d, G)) for d in range(1, G)]
+        mhi[l, :, at] = hi
+        mlo[l, :, at] = lo
 
     def apply(a, l, dims):
         hi, lo = split(a)
@@ -179,7 +222,10 @@
         gram = jnp.zeros((K, K), F32)
         for g in range(G):
             pg = whole_p(g)
-            gram = gram + dot(pg, pg, NT, HIGH)
+            hi, lo = split(pg)
+            both = jnp.concatenate([hi, lo], axis=0)
+            both = dot(both, both, NT)
+            gram = gram + (both[:K, :K] + both[:K, K:] + both[K:, :K])
         gram = gram * same
         squares = jnp.sum(gram * gram, axis=1, keepdims=True)
         fro = jnp.zeros((K, 1), F32)
@@ -191,11 +237,13 @@
 
         def newton(ymat, zmat, count):
             for _ in range(count):
-                tmat = 1.5 * eye - 0.5 * dot(zmat, ymat, NN, HIGH)
-                ymat = dot(ymat, tmat, NN, HIGH)
-                zmat = dot(tmat, zmat, NN, HIGH)
+                tmat = 1.5 * eye - 0.5 * dot3(zmat, ymat)
+                ymat = dot3(ymat, tmat)
+                zmat = dot3(tmat, zmat)
             return ymat, zmat
 
+        if rnd == 0:
+            w_last(w_x)
         ymat, zmat = newton(ymat, zmat, 1)
         wait(copies)
         tmid[rnd] = jnp.sum(trs[rnd], axis=0)
@@ -210,30 +258,25 @@
         wait(over_grp(4 + 3 * rnd, lambda g: tag.at[rnd, me_g], tag.at[rnd, me_g]))
         t = jnp.concatenate([tag[rnd, i // R, i % R] for i in range(G * R)], axis=0)[:K]
         inv = 1.0 / jnp.sqrt(fro)
-        qall = dot(zmat, t, TN, HIGH) * inv
+        qall = factors(zmat, t) * inv
         q = [qall[l * rank:(l + 1) * rank] for l in range(L)]
         if rnd == ROUNDS - 1:
             q_out[...] = qall
             for g in range(G):
-                phat_out[g] = dot(zmat, whole_p(g), TN, HIGH) * inv
+                phat_out[g] = factors(zmat, whole_p(g)) * inv
 
     wait(bias_copies)
     wait(small_copies)
     bias_out[...] = jnp.sum(bgrp[...], axis=0)
     small_out[...] = bsmall[...]
-    for l in range(L):
-        core_copies[l].wait_send()
-        for copy in y_copies[l]:
+    for u in range(len(units)):
+        core_copies[u].wait_send()
+        for copy in y_copies[u]:
             copy.wait_send()
     local_w.wait()
-    wait(w_copies)
-
-
-def factors(ph, q):
-    ph_hi, ph_lo = split(ph)
-    q_hi, q_lo = split(q)
-    return dot(jnp.concatenate([ph_hi, ph_hi, ph_lo], axis=0),
-               jnp.concatenate([q_hi, q_lo, q_hi], axis=0), TN)
+    for copy in w_y + w_x:
+        copy.wait_send()
+    wait(w_rest)
 
 
 def weights_kernel(reps, ph, q, w, out):
@@ -259,13 +302,15 @@
     pp = -(-K // R)
     pr = -(-K // (G * R))
     chunk = 384 if width % 384 == 0 else 128
+    cut = width // 256 // 2 * 256
+    pieces = ((0, cut), (cut, width - cut))
     bias_in = jnp.concatenate([bias_momenta, biases.astype(F32)], axis=0)
     vm = pl.BlockSpec(memory_space=pltpu.VMEM)
     hbm = pl.BlockSpec(memory_space=pl.ANY)
     dma = pltpu.SemaphoreType.DMA
     n_rep, n_grp = 1 + 4 * ROUNDS, 2 + 3 * ROUNDS
     merged, phat, q, w_all, bias_sum, small = pl.pallas_call(
-        functools.partial(step_kernel, (L, G, R, rank, width, tok, chunk)),
+        functools.partial(step_kernel, (L, G, R, rank, width, tok, chunk, pieces)),
         out_shape=(
             jax.ShapeDtypeStruct((L, rows, width), F32),
             jax.ShapeDtypeStruct((G, K, rows), F32),
@@ -299,9 +344,9 @@
             pltpu.VMEM((G, L, width), F32),
             pltpu.VMEM((G, 2 * L, rows), F32),
             dma((2 * L + 1,)),
-            dma((L,)), dma((L,)),
-            dma((L, Y - 1)), dma((L, Y - 1)),
-            dma((G - 1,)), dma((G - 1,)),
+            dma((2 * L,)), dma((2 * L,)),
+            dma((2 * L, Y - 1)), dma((2 * L, Y - 1)),
+            dma((4, Y)), dma((4, Y)),
             dma((n_rep, R - 1)), dma((n_rep, R - 1)),
             dma((n_grp, G - 1)), dma((n_grp, G - 1)),
         ],

time: 190 us -> 140 us (0.74)
  Pallas kernels: 178 us -> 128 us
    pallas_call x1, Pallas kernels: 170 us -> 120 us  [body(): pl.pallas_call(functools.partial(step_kernel, (L, G, R, rank, width, tok,...]
where the time goes in v2:
time: 140 us; the launch traced here: 139 us
  Pallas kernels  128 us (91%)
  local copies, waits for them, and re-layouts  7.95 us (6%)
  other arithmetic  2.59 us (2%)
    pallas_call x1, Pallas kernels, body(): pl.pallas_call(functools.partial(step_kernel, (L, G, R, rank, width, tok,...  120 us
    unnamed x16, local copies, waits for them, and re-layouts  6.21 us
    pallas_call x1, Pallas kernels, body(): pl.pallas_call(functools.partial(weights_kernel, R), out_shape=jax.ShapeD...  5.37 us

profile of v2, /device:TPU:1, one launch (start us, length us, event | category | flops | bytes accessed | tf_op | source)
XLA Modules:
  0.0 139.2 jit_solution(10244093586962384571)
XLA Ops:
  0.6 0.7 convert_element_type.6
  1.3 1.3 pad_maximum_fusion.bias_in
  2.6 119.8 %shard_map.119 = (f32[2,288,1152]{2,1,0:T(8,128)}, f32[4,64,288]{2,1,0:T(8,128)}, f32[64,1152]{1,0:T(8,128)}, bf16[4,2,288,1152]{3,2,1,0:T(8,128)(2,1)}, f32[2,1152]{1,0:T(2,128)}, /*index=5*/f32[4,4,288]{2,1,0:T(4,128)}) custom-call(bf16[2,2048,1152]{2,1,0:T(8,128)(2,1)} %x_hbm.1, bf16[2,2048,1152]{2,1,0:T(8,128)(2,1)} %y_hbm.1, f32[2,288,1152]{2,1,0:T(8,128)} %bitcast.12, ...), custom_call_target="tpu_custom_call" | custom-call | flops 10871635968 | bytes 18874368 | tf_op jit(solution)/shard_map/pallas_call | solution.py:312
  122.4 0.0 copy-start
  122.4 2.5 %copy-done = bf16[4,2,288,1152]{3,2,1,0:T(8,128)(2,1)S(1)} copy-done((bf16[4,2,288,1152]{3,2,1,0:T(8,128)(2,1)S(1)}, bf16[4,2,288,1152]{3,2,1,0:T(8,128)(2,1)}, u32[]{:S(2)}) %copy-start) | copy-done | bytes 5308440
  124.9 0.0 copy-start.3
  124.9 1.0 copy-done.3
  125.8 0.0 copy-start.5
  125.8 1.0 copy-done.5
  126.8 0.0 copy-start.6
  126.8 0.0 copy-start.7
  126.8 0.0 copy-start.1
  126.8 0.0 copy-start.4
  126.9 5.4 %shard_map.120 = bf16[2,1152,1152]{2,1,0:T(8,128)(2,1)} custom-call(f32[4,2,32,288]{3,2,1,0:T(8,128)S(1)} %bitcast.9, f32[2,32,1152]{2,1,0:T(8,128)S(1)} %bitcast.7, bf16[4,2,288,1152]{3,2,1,0:T(8,128)(2,1)S(1)} %copy-done), custom_call_target="tpu_custom_call" | custom-call | tf_op jit(solution)/shard_map/pallas_call | solution.py:359
  132.2 0.0 copy-done.6
  132.3 0.1 slice.11
  132.4 0.1 mul.26
  132.4 0.0 copy-done.7
  132.5 0.6 subtract_convert_fusion
  133.1 0.9 constant_dynamic-slice_fusion.1
  134.0 0.0 copy-done.1
  134.0 0.0 copy-done.4
  134.0 0.0 copy-start.2
  134.0 1.7 %copy-done.2 = f32[2,288,1152]{2,1,0:T(8,128)S(1)} copy-done((f32[2,288,1152]{2,1,0:T(8,128)S(1)}, f32[2,288,1152]{2,1,0:T(8,128)}, u32[]{:S(2)}) %copy-start.2) | copy-done | bytes 2654232
  135.7 2.8 %shard_map.121 = (f32[2,288,1152]{2,1,0:T(8,128)}, f32[2,288,1152]{2,1,0:T(8,128)}) custom-call(f32[2,32,288]{2,1,0:T(8,128)S(1)} %bitcast.10, f32[2,32,1152]{2,1,0:T(8,128)S(1)} %bitcast.8, f32[2,288,1152]{2,1,0:T(8,128)S(1)} %copy-done.2, f32[2,288,1152]{2,1,0:T(8,128)S(1)} %copy-done.1), custom_call_target="tpu_custom_call" | custom-call | tf_op jit(solution)/shard_map/pallas_call | solution.py:374
  138.5 0.7 constant_dynamic-slice_fusion
  (3 shorter events, 0.0 us)
Async XLA Ops:
  122.4 2.5 %copy-start = (bf16[4,2,288,1152]{3,2,1,0:T(8,128)(2,1)S(1)}, bf16[4,2,288,1152]{3,2,1,0:T(8,128)(2,1)}, u32[]{:S(2)}) copy-start(bf16[4,2,288,1152]{3,2,1,0:T(8,128)(2,1)} %get-tuple-element.15.w) | copy-start | bytes 15925252
  124.9 1.0 copy-start.3
  125.8 1.0 copy-start.5
  126.8 5.4 %copy-start.6 = (f32[4,4,288]{2,1,0:T(4,128)S(1)}, f32[4,4,288]{2,1,0:T(4,128)}, u32[]{:S(2)}) copy-start(f32[4,4,288]{2,1,0:T(4,128)} %get-tuple-element.16) | copy-start | bytes 55300
  126.8 5.6 %copy-start.7 = (f32[2,1152]{1,0:T(2,128)S(1)}, f32[2,1152]{1,0:T(2,128)}, u32[]{:S(2)}) copy-start(f32[2,1152]{1,0:T(2,128)} %get-tuple-element.17) | copy-start | bytes 27652
  126.8 7.1 %copy-start.1 = (f32[2,288,1152]{2,1,0:T(8,128)S(1)}, f32[2,288,1152]{2,1,0:T(8,128)}, u32[]{:S(2)}) copy-start(f32[2,288,1152]{2,1,0:T(8,128)} %momenta.3) | copy-start | bytes 7962628
  126.8 7.1 %copy-start.4 = (f32[64,1152]{1,0:T(8,128)S(1)}, f32[64,1152]{1,0:T(8,128)}, u32[]{:S(2)}) copy-start(f32[64,1152]{1,0:T(8,128)} %get-tuple-element.14) | copy-start | bytes 884740
  134.0 1.8 %copy-start.2 = (f32[2,288,1152]{2,1,0:T(8,128)S(1)}, f32[2,288,1152]{2,1,0:T(8,128)}, u32[]{:S(2)}) copy-start(f32[2,288,1152]{2,1,0:T(8,128)} %get-tuple-element.18.merged) | copy-start | bytes 7962628
